TPU v7x, 512 devices: a whole 4x8x8 slice. The times are simulated.
512 devices in a mesh: dom: 128 (over z, y, core), grp: 4 (over x).
Axes of the slice: x: 4, y: 8, z: 8, core: 2. Of those that a mesh axis runs over, the one named last changes fastest.
Arguments:
- source_emb: float32 [400, 65536], P(None, ('dom', 'grp')), may hold values from -2.5 to 2.5
- source_state: float32 [65536], P(('dom', 'grp')), may hold values from 0.005 to 0.1
- dest_emb: float32 [400, 65536], P(None, ('dom', 'grp')), may hold values from -2.5 to 2.5
- dest_state: float32 [65536], P(('dom', 'grp')), may hold values from 0.005 to 0.1
- relations: float32 [400, 768], replicated, may hold values from -4 to 4
- relation_state: float32 [768], replicated, may hold values from 1 to 30
- partner: int32 [128, 4], P('dom', 'grp'), may hold values from 0 to 127, as said below
- edge_count: int32 [128, 4], P('dom', 'grp'), may hold values from 1 to 1024, as said below
- source_rows: int32 [128, 4, 1024], P('dom', 'grp'), may hold values from 0 to 127
- target_rows: int32 [128, 4, 1024], P('dom', 'grp'), may hold values from 0 to 127
- relation_index: int32 [128, 4, 1024], P('dom', 'grp'), may hold values from 0 to 767
- negative_rows: int32 [128, 4, 2048], P('dom', 'grp'), may hold values from 0 to 127
Outputs:
- source_out: float32 [400, 65536], P(None, ('dom', 'grp'))
- source_state_out: float32 [65536], P(('dom', 'grp'))
- dest_out: float32 [400, 65536], P(None, ('dom', 'grp'))
- dest_state_out: float32 [65536], P(('dom', 'grp'))
- relations_out: float32 [400, 768], replicated
- relation_state_out: float32 [768], replicated
Inputs may be any that keep to these rules, and one draw needn't show every extreme that they name: For each grp index g, partner[:, g] is a permutation of 0 .. 127. `edge_count`: some device has all 1024 edges live.
All inputs are finite; a program needn't handle non-finite values.
Results may differ from a plain program's by a relative error of at most 0.0013.
The roundings to bfloat16 on the way count: a program that leaves them out, or rounds other values in their place, can miss the bound.
Values sent between devices are 32-bit elements; how exact they have to be, the bound alone decides.
No kernel may reach another device: no remote copies, remote signals or barrier semaphores. Data moves between devices by JAX's collectives and lax.ppermute only.
A program may use at most 64 MiB of HBM per device.

v0:
```python
import jax
import jax.numpy as jnp
from jax import lax
from jax.sharding import PartitionSpec as P

SPAN = 512
SPANS = 2
NEG = 1024
EDGES = 1024
learn_rate = 0.3
epsilon = 1e-08


def passed_along(value, axis, steps):
    count = lax.axis_size(axis)
    pairs = [(source, (source + steps) % count) for source in range(count)]
    return lax.ppermute(value, axis, pairs)


def adagrad(param, state, grad):
    new_state = state + jnp.mean(grad * grad, axis=0)
    return (param - learn_rate * grad / (jnp.sqrt(new_state) + epsilon), new_state)


def contract_last(left, right):
    return lax.dot_general(
        left, right, (((1,), (1,)), ((), ())), preferred_element_type=jnp.float32
    )


def selector(count, rows):
    return (jnp.arange(count, dtype=jnp.int32)[:, None] == rows[None, :]).astype(jnp.bfloat16)


def train_block(
    source, source_acc, target, target_acc, relation_bf, rows_s, rows_t, rows_r, rows_n, live
):
    width = source.shape[0]
    half = width // 2
    block = source.shape[1]
    pick_source = selector(block, rows_s)
    pick_target = selector(block, rows_t)
    pick_noise = selector(block, rows_n)
    pick_relation = selector(relation_bf.shape[1], rows_r)
    source_bf = source.astype(jnp.bfloat16)
    target_bf = target.astype(jnp.bfloat16)
    subject = jnp.dot(source_bf, pick_source, preferred_element_type=jnp.float32)
    operator = jnp.dot(relation_bf, pick_relation, preferred_element_type=jnp.float32)
    objects = jnp.dot(target_bf, pick_target, preferred_element_type=jnp.float32)
    noise = jnp.dot(target_bf, pick_noise, preferred_element_type=jnp.float32).astype(jnp.bfloat16)
    subject_re, subject_im = (subject[:half], subject[half:])
    operator_re, operator_im = (operator[:half], operator[half:])
    query = jnp.concatenate(
        [
            subject_re * operator_re - subject_im * operator_im,
            subject_re * operator_im + subject_im * operator_re,
        ],
        0,
    )
    positive = jnp.sum(query * objects, axis=0)
    query_bf = query.astype(jnp.bfloat16)
    negative = lax.dot_general(
        query_bf, noise, (((0,), (0,)), ((), ())), preferred_element_type=jnp.float32
    )
    grad_pos = -jax.nn.sigmoid(-positive) * live
    grad_neg = (jax.nn.sigmoid(negative) * (live[:, None] / NEG)).astype(jnp.bfloat16)
    grad_query = grad_pos[None, :] * objects + contract_last(noise, grad_neg)
    grad_objects = grad_pos[None, :] * query
    grad_noise = jnp.dot(query_bf, grad_neg, preferred_element_type=jnp.float32)
    query_gre, query_gim = (grad_query[:half], grad_query[half:])
    grad_subject = jnp.concatenate(
        [
            query_gre * operator_re + query_gim * operator_im,
            query_gim * operator_re - query_gre * operator_im,
        ],
        0,
    )
    grad_operator = jnp.concatenate(
        [
            query_gre * subject_re + query_gim * subject_im,
            query_gim * subject_re - query_gre * subject_im,
        ],
        0,
    )
    grad_source = contract_last(grad_subject.astype(jnp.bfloat16), pick_source)
    grad_target = contract_last(grad_objects.astype(jnp.bfloat16), pick_target)
    grad_target = grad_target + contract_last(grad_noise.astype(jnp.bfloat16), pick_noise)
    grad_local = contract_last(grad_operator.astype(jnp.bfloat16), pick_relation)
    new_source, new_source_acc = adagrad(source, source_acc, grad_source)
    new_target, new_target_acc = adagrad(target, target_acc, grad_target)
    return (new_source, new_source_acc, new_target, new_target_acc, grad_local)


def relation_step(relations, relation_state, grad_local):
    total = lax.psum(grad_local, ("dom", "grp"))
    return adagrad(relations, relation_state, total)


def local(
    source_emb,
    source_state,
    dest_emb,
    dest_state,
    relations,
    relation_state,
    partner,
    edge_count,
    source_rows,
    target_rows,
    relation_index,
    negative_rows,
):
    width = source_emb.shape[0]
    block = source_emb.shape[1]
    members = lax.axis_size("dom")
    piece = block // members
    cargo = jnp.concatenate([dest_emb, dest_state[None, :]], 0)
    cargo = passed_along(cargo, "grp", 1)
    partners = lax.all_gather(partner[0], "dom", axis=0, tiled=True)
    spread = lax.all_to_all(
        cargo.reshape(width + 1, members, piece), "dom", split_axis=1, concat_axis=1, tiled=True
    )
    spread = jnp.take(spread, partners, axis=1)
    arrived = lax.all_to_all(spread, "dom", split_axis=1, concat_axis=1, tiled=True).reshape(
        width + 1, block
    )
    target = arrived[:width]
    target_acc = arrived[width]
    source = source_emb
    source_acc = source_state
    live_all = (jnp.arange(EDGES, dtype=jnp.int32) < edge_count[0, 0]).astype(jnp.float32)
    for step in range(SPANS):
        first = step * SPAN
        first_neg = step * NEG
        relation_bf = relations.astype(jnp.bfloat16)
        source, source_acc, target, target_acc, grad_local = train_block(
            source,
            source_acc,
            target,
            target_acc,
            relation_bf,
            source_rows[0, 0, first : first + SPAN],
            target_rows[0, 0, first : first + SPAN],
            relation_index[0, 0, first : first + SPAN],
            negative_rows[0, 0, first_neg : first_neg + NEG],
            live_all[first : first + SPAN],
        )
        relations, relation_state = relation_step(relations, relation_state, grad_local)
    cargo = jnp.concatenate([target, target_acc[None, :]], 0).reshape(width + 1, members, piece)
    collected = lax.all_to_all(cargo, "dom", split_axis=1, concat_axis=1, tiled=True)
    inverse = (
        jnp.zeros((members,), jnp.int32).at[partners].set(jnp.arange(members, dtype=jnp.int32))
    )
    collected = jnp.take(collected, inverse, axis=1)
    returned = lax.all_to_all(collected, "dom", split_axis=1, concat_axis=1, tiled=True).reshape(
        width + 1, block
    )
    settled = passed_along(returned, "grp", -1)
    return (source, source_acc, settled[:width], settled[width], relations, relation_state)


def solution(mesh):
    in_specs = (
        P(None, ("dom", "grp")),
        P(("dom", "grp")),
        P(None, ("dom", "grp")),
        P(("dom", "grp")),
        P(),
        P(),
        P("dom", "grp"),
        P("dom", "grp"),
        P("dom", "grp", None),
        P("dom", "grp", None),
        P("dom", "grp", None),
        P("dom", "grp", None),
    )
    out_specs = (
        P(None, ("dom", "grp")),
        P(("dom", "grp")),
        P(None, ("dom", "grp")),
        P(("dom", "grp")),
        P(),
        P(),
    )
    return jax.shard_map(local, mesh=mesh, in_specs=in_specs, out_specs=out_specs, check_vma=False)
```

profile of v0, /device:TPU:23, one launch (start us, length us, event | category | flops | bytes accessed | tf_op | source)
XLA Modules:
  0.0 705.2 jit_solution(11849376523727967690)
XLA Ops:
  8.2 2.1 collective-permute-start
  11.0 1.3 dynamic-slice
  13.0 27.1 %all-reduce = s32[128]{0:T(128)S(1)} all-reduce(s32[128]{0:T(128)S(1)} %bitcast_dynamic-update-slice_fusion), channel_id=2, replica_groups=mesh['dom'=128,'grp'=4] {'dom'}, use_global_device_ids=true, to_apply=%add | all-reduce | flops 128 | bytes 1024 | tf_op jit(solution)/shard_map/all_gather | solution.py:119
  43.8 1.2 convolution_bitcast_fusion
  45.9 11.1 %all-to-all-start = ((f32[401,128,1]{0,2,1:T(1,128)}), f32[401,128,1]{0,2,1:T(1,128)S(1)}, u32[]{:S(2)}, u32[]{:S(2)}) async-start(f32[401,128,1]{0,2,1:T(1,128)} %copy.35), calls=%async_computation | async-start | bytes 524288 | tf_op jit(solution)/shard_map/all_to_all | solution.py:120
  58.2 11.9 %all-to-all-done = f32[401,128,1]{0,2,1:T(1,128)S(1)} async-done(((f32[401,128,1]{0,2,1:T(1,128)}), f32[401,128,1]{0,2,1:T(1,128)S(1)}, u32[]{:S(2)}, u32[]{:S(2)}) %all-to-all-start) | async-done | bytes 205344 | tf_op jit(solution)/shard_map/all_to_all | solution.py:120
  71.9 8.8 %all-to-all-start.1 = ((f32[401,128,1]{0,2,1:T(1,128)}), f32[401,128,1]{0,2,1:T(1,128)}, u32[]{:S(2)}, u32[]{:S(2)}) async-start(f32[401,128,1]{0,2,1:T(1,128)} %copy.38), calls=%async_computation.1 | async-start | bytes 524288 | tf_op jit(solution)/shard_map/all_to_all | solution.py:124
  81.9 11.6 %all-to-all-done.1 = f32[401,128,1]{0,2,1:T(1,128)} async-done(((f32[401,128,1]{0,2,1:T(1,128)}), f32[401,128,1]{0,2,1:T(1,128)}, u32[]{:S(2)}, u32[]{:S(2)}) %all-to-all-start.1) | async-done | bytes 205344 | tf_op jit(solution)/shard_map/all_to_all | solution.py:124
  93.5 1.1 copy.47
  95.6 1.2 multiply_reduce_fusion.3
  97.8 2.0 multiply_convert_fusion.1
  99.8 2.9 multiply_reduce_fusion.6
  102.7 2.3 convolution_add_fusion.1
  105.4 1.6 fusion.2
  107.3 2.7 slice_reduce_fusion
  110.1 1.3 convolution_convert_fusion.1
  111.7 264.1 %all-reduce.4.cloned.1.call-done = f32[400,768]{1,0:T(8,128)} async-done(((f32[400,768]{1,0:T(8,128)}), f32[400,768]{1,0:T(8,128)}) %all-reduce.4.cloned.1.call-update) | async-done | bytes 1228816 | tf_op jit(solution)/shard_map/psum | solution.py:95
  375.8 1.5 multiply_reduce_fusion.1
  379.0 1.2 multiply_reduce_fusion.2
  381.2 2.0 multiply_convert_fusion
  383.2 3.0 multiply_reduce_fusion.4
  386.2 2.4 convolution_add_fusion
  388.6 1.3 add_convert_fusion
  390.8 9.6 %all-to-all-start.2 = ((f32[401,128,1]{0,2,1:T(1,128)}), f32[401,128,1]{0,2,1:T(1,128)S(1)}, u32[]{:S(2)}, u32[]{:S(2)}) async-start(f32[401,128,1]{0,2,1:T(1,128)} %copy.40), calls=%async_computation.2 | async-start | bytes 524288 | tf_op jit(solution)/shard_map/all_to_all | solution.py:150
  400.5 2.6 fusion
  403.9 9.6 %all-to-all-done.2 = f32[401,128,1]{0,2,1:T(1,128)S(1)} async-done(((f32[401,128,1]{0,2,1:T(1,128)}), f32[401,128,1]{0,2,1:T(1,128)S(1)}, u32[]{:S(2)}, u32[]{:S(2)}) %all-to-all-start.2) | async-done | bytes 205344 | tf_op jit(solution)/shard_map/all_to_all | solution.py:150
  415.3 7.7 %all-to-all-start.3 = ((f32[401,128,1]{0,2,1:T(1,128)}), f32[401,128,1]{0,2,1:T(1,128)S(1)}, u32[]{:S(2)}, u32[]{:S(2)}) async-start(f32[401,128,1]{0,2,1:T(1,128)} %copy.43), calls=%async_computation.3 | async-start | bytes 524288 | tf_op jit(solution)/shard_map/all_to_all | solution.py:155
  423.8 261.1 %all-reduce.6.cloned.1.call-done = f32[400,768]{1,0:T(8,128)} async-done(((f32[400,768]{1,0:T(8,128)}), f32[400,768]{1,0:T(8,128)}) %all-reduce.6.cloned.1.call-update) | async-done | bytes 1228816 | tf_op jit(solution)/shard_map/psum | solution.py:95
  684.9 1.4 multiply_reduce_fusion
  687.0 2.3 collective-permute-start.1
  689.3 2.6 divide_subtract_fusion
  691.9 5.2 collective-permute-done.1
  (99 shorter events, 21.8 us)
Async XLA Ops:
  7.2 50.5 %copy-start = (f32[400,768]{1,0:T(8,128)S(1)}, f32[400,768]{1,0:T(8,128)}, u32[]{:S(2)}) copy-start(f32[400,768]{1,0:T(8,128)} %param.18) | copy-start | bytes 3686404
  8.2 36.8 %collective-permute-start = (f32[401,128]{1,0:T(8,128)S(1)}, f32[401,128]{1,0:T(8,128)S(1)}, u32[]{:S(2)}, u32[]{:S(2)}) collective-permute-start(f32[401,128]{1,0:T(8,128)S(1)} %pad_maximum_fusion.2), channel_id=1, source_target_pairs={{0,1},{1,2},{2,3},{3,0},{4,5},{5,6},{6,7},{7,4},{8,9},{9,10},{10,1... | collective-permute-start | bytes 615944 | tf_op jit(solution)/shard_map/ppermute | solution.py:17
  45.9 24.2 %all-to-all-start = ((f32[401,128,1]{0,2,1:T(1,128)}), f32[401,128,1]{0,2,1:T(1,128)S(1)}, u32[]{:S(2)}, u32[]{:S(2)}) async-start(f32[401,128,1]{0,2,1:T(1,128)} %copy.35), calls=%async_computation | async-start | bytes 524288 | tf_op jit(solution)/shard_map/all_to_all | solution.py:120
  71.9 21.6 %all-to-all-start.1 = ((f32[401,128,1]{0,2,1:T(1,128)}), f32[401,128,1]{0,2,1:T(1,128)}, u32[]{:S(2)}, u32[]{:S(2)}) async-start(f32[401,128,1]{0,2,1:T(1,128)} %copy.38), calls=%async_computation.1 | async-start | bytes 524288 | tf_op jit(solution)/shard_map/all_to_all | solution.py:124
  80.7 295.1 %all-reduce.4.cloned.1.call-start = ((), (), s32[]{:S(2)}) async-start(), calls=%async_computation.4 | async-start | bytes 2457600 | tf_op jit(solution)/shard_map/psum | solution.py:95
  94.6 1.0 copy-start.8
  95.0 2.8 copy-start.5
  106.9 3.1 copy-start.16
  107.0 3.1 copy-start.19
  107.0 4.4 copy-start.6
  107.3 4.1 copy-start.11
  111.4 265.9 %copy-start.18 = (f32[768]{0:T(1024)S(1)}, f32[768]{0:T(1024)}, u32[]{:S(2)}) copy-start(f32[768]{0:T(1024)} %param.19) | copy-start | bytes 9220
  375.8 1.7 copy-start.1
  378.1 0.9 copy-start.2
  378.3 2.9 copy-start.9
  378.3 2.9 copy-start.10
  379.0 2.2 copy-start.4
  386.2 2.4 copy-start.3
  388.6 1.3 copy-start.17
  389.9 10.5 %copy-start.15 = (bf16[200,512]{1,0:T(8,128)(2,1)S(1)}, bf16[200,512]{1,0:T(8,128)(2,1)}, u32[]{:S(2)}) copy-start(bf16[200,512]{1,0:T(8,128)(2,1)} %get-tuple-element.29) | copy-start | bytes 614404
  390.8 22.6 %all-to-all-start.2 = ((f32[401,128,1]{0,2,1:T(1,128)}), f32[401,128,1]{0,2,1:T(1,128)S(1)}, u32[]{:S(2)}, u32[]{:S(2)}) async-start(f32[401,128,1]{0,2,1:T(1,128)} %copy.40), calls=%async_computation.2 | async-start | bytes 524288 | tf_op jit(solution)/shard_map/all_to_all | solution.py:150
  400.4 284.5 %all-reduce.6.cloned.1.call-start = ((), (), s32[]{:S(2)}) async-start(), calls=%async_computation.5 | async-start | bytes 2457600 | tf_op jit(solution)/shard_map/psum | solution.py:95
  400.4 2.6 copy-start.13
  400.4 2.6 copy-start.14
  414.2 8.8 %copy-start.7 = (f32[400,128]{1,0:T(8,128)S(1)}, f32[400,128]{1,0:T(8,128)}, u32[]{:S(2)}) copy-start(f32[400,128]{1,0:T(8,128)} %param.14) | copy-start | bytes 614404
  414.2 8.8 %copy-start.12 = (f32[400,128]{1,0:T(8,128)S(1)}, f32[400,128]{1,0:T(8,128)}, u32[]{:S(2)}) copy-start(f32[400,128]{1,0:T(8,128)} %copy-done.11) | copy-start | bytes 614404
  415.3 271.6 %all-to-all-start.3 = ((f32[401,128,1]{0,2,1:T(1,128)}), f32[401,128,1]{0,2,1:T(1,128)S(1)}, u32[]{:S(2)}, u32[]{:S(2)}) async-start(f32[401,128,1]{0,2,1:T(1,128)} %copy.43), calls=%async_computation.3 | async-start | bytes 524288 | tf_op jit(solution)/shard_map/all_to_all | solution.py:155
  687.0 10.1 %collective-permute-start.1 = (f32[401,128]{1,0:T(8,128)S(1)}, f32[401,128]{1,0:T(8,128)S(1)}, u32[]{:S(2)}, u32[]{:S(2)}) collective-permute-start(f32[401,128]{1,0:T(8,128)S(1)} %bitcast.84), channel_id=1, source_target_pairs={{0,3},{1,0},{2,1},{3,2},{4,7},{5,4},{6,5},{7,6},{8,11},{9,8},{10,9... | collective-permute-start | bytes 615944 | tf_op jit(solution)/shard_map/ppermute | solution.py:17
Sparse Core Ops, SparseCore 0:
  107.1 268.6 all-reduce.3
  407.7 277.1 all-reduce.5
where the time goes:
time: 706 us; the launch traced here: 705 us
  waiting for transfers between devices  564 us (80%)
  starting transfers between devices  41.8 us (6%)
  matrix products  27.9 us (4%)
  blocking collectives  27.1 us (4%)
  local copies, waits for them, and re-layouts  17.5 us (2%)
  between operations  15.8 us (2%)
  other arithmetic  11.5 us (2%)
    psum x2, waiting for transfers between devices, relation_step(): total = lax.psum(grad_local, ('dom', 'grp'))  525 us
    all_gather x1, blocking collectives, local(): partners = lax.all_gather(partner[0], 'dom', axis=0, tiled=True)  27.1 us
    dot_general x10, matrix products, contract_last(): lax.dot_general(left, right, (((1,), (1,)), ((), ())), preferred_element_...  17.3 us
  transfers between devices with their start and end apart: 8, of which 6 were waited for; matrix products, arithmetic and copies ran while one was open for 3% of the time, Pallas kernels for 0%

commit v1 on v0

--- a/solution.py
+++ b/solution.py
@@ -92,7 +92,7 @@
 
 
 def relation_step(relations, relation_state, grad_local):
-    total = lax.psum(grad_local, ("dom", "grp"))
+    total = lax.psum(lax.psum(grad_local, "grp"), "dom")
     return adagrad(relations, relation_state, total)
 
 

time: 706 us -> 642 us (0.909)
  the two profiles are of different devices: /device:TPU:23 before, /device:TPU:24 now
where the time goes in v1:
time: 642 us; the launch traced here: 641 us
  waiting for transfers between devices  499 us (78%)
  starting transfers between devices  40.2 us (6%)
  blocking collectives  31 us (5%)
  matrix products  23.2 us (4%)
  local copies, waits for them, and re-layouts  18.8 us (3%)
  between operations  15.7 us (2%)
  other arithmetic  13.3 us (2%)
    psum x4, waiting for transfers between devices, relation_step(): total = lax.psum(lax.psum(grad_local, 'grp'), 'dom')  461 us
    all_gather x1, blocking collectives, local(): partners = lax.all_gather(partner[0], 'dom', axis=0, tiled=True)  31 us
    dot_general x10, matrix products, contract_last(): lax.dot_general(left, right, (((1,), (1,)), ((), ())), preferred_element_...  14.3 us
    all_to_all x1, waiting for transfers between devices, local(): lax.all_to_all(cargo, 'dom', split_axis=1, concat_axis=1, tiled=True)  12.9 us
  transfers between devices with their start and end apart: 10, of which 8 were waited for; matrix products, arithmetic and copies ran while one was open for 4% of the time, Pallas kernels for 0%

profile of v1, /device:TPU:24, one launch (start us, length us, event | category | flops | bytes accessed | tf_op | source)
XLA Modules:
  0.0 640.9 jit_solution(14024914731652758289)
XLA Ops:
  8.2 3.4 collective-permute-start
  12.3 1.3 dynamic-slice
  14.2 31.0 %all-reduce = s32[128]{0:T(128)S(1)} all-reduce(s32[128]{0:T(128)S(1)} %bitcast_dynamic-update-slice_fusion), channel_id=2, replica_groups=mesh['dom'=128,'grp'=4] {'dom'}, use_global_device_ids=true, to_apply=%add | all-reduce | flops 128 | bytes 1024 | tf_op jit(solution)/shard_map/all_gather | solution.py:119
  47.3 1.2 convolution_bitcast_fusion
  49.4 7.3 %all-to-all-start = ((f32[401,128,1]{0,2,1:T(1,128)}), f32[401,128,1]{0,2,1:T(1,128)}, u32[]{:S(2)}, u32[]{:S(2)}) async-start(f32[401,128,1]{0,2,1:T(1,128)} %copy.35), calls=%async_computation | async-start | bytes 524288 | tf_op jit(solution)/shard_map/all_to_all | solution.py:120
  57.3 12.0 %all-to-all-done = f32[401,128,1]{0,2,1:T(1,128)} async-done(((f32[401,128,1]{0,2,1:T(1,128)}), f32[401,128,1]{0,2,1:T(1,128)}, u32[]{:S(2)}, u32[]{:S(2)}) %all-to-all-start) | async-done | bytes 205344 | tf_op jit(solution)/shard_map/all_to_all | solution.py:120
  70.3 1.5 gather_fusion
  73.8 9.0 %all-to-all-start.1 = ((f32[401,128,1]{0,2,1:T(1,128)}), f32[401,128,1]{0,2,1:T(1,128)}, u32[]{:S(2)}, u32[]{:S(2)}) async-start(f32[401,128,1]{0,2,1:T(1,128)} %copy.38), calls=%async_computation.1 | async-start | bytes 524288 | tf_op jit(solution)/shard_map/all_to_all | solution.py:124
  85.4 10.0 %all-to-all-done.1 = f32[401,128,1]{0,2,1:T(1,128)} async-done(((f32[401,128,1]{0,2,1:T(1,128)}), f32[401,128,1]{0,2,1:T(1,128)}, u32[]{:S(2)}, u32[]{:S(2)}) %all-to-all-start.1) | async-done | bytes 205344 | tf_op jit(solution)/shard_map/all_to_all | solution.py:124
  100.9 1.6 fusion.2
  102.8 2.7 slice_reduce_fusion
  105.8 2.1 multiply_reduce_fusion.6
  108.3 46.7 %all-reduce.6.cloned.1.call-done = f32[400,768]{1,0:T(8,128)} async-done(((f32[400,768]{1,0:T(8,128)}), f32[400,768]{1,0:T(8,128)}) %all-reduce.6.cloned.1.call-update) | async-done | bytes 1228816 | tf_op jit(solution)/shard_map/psum | solution.py:95
  155.1 1.3 convolution_convert_fusion.1
  156.7 201.9 %all-reduce.8.cloned.1.call-done = f32[400,768]{1,0:T(8,128)} async-done(((f32[400,768]{1,0:T(8,128)}), f32[400,768]{1,0:T(8,128)}) %all-reduce.8.cloned.1.call-update) | async-done | bytes 1228816 | tf_op jit(solution)/shard_map/psum | solution.py:95
  358.6 1.5 multiply_reduce_fusion.1
  361.7 1.2 multiply_reduce_fusion.2
  364.0 2.0 multiply_convert_fusion
  365.9 3.0 multiply_reduce_fusion.4
  368.9 2.4 convolution_add_fusion
  372.5 1.6 fusion
  375.0 8.5 %all-to-all-start.2 = ((f32[401,128,1]{0,2,1:T(1,128)}), f32[401,128,1]{0,2,1:T(1,128)S(1)}, u32[]{:S(2)}, u32[]{:S(2)}) async-start(f32[401,128,1]{0,2,1:T(1,128)} %copy.40), calls=%async_computation.2 | async-start | bytes 524288 | tf_op jit(solution)/shard_map/all_to_all | solution.py:150
  383.5 12.9 %all-to-all-done.2 = f32[401,128,1]{0,2,1:T(1,128)S(1)} async-done(((f32[401,128,1]{0,2,1:T(1,128)}), f32[401,128,1]{0,2,1:T(1,128)S(1)}, u32[]{:S(2)}, u32[]{:S(2)}) %all-to-all-start.2) | async-done | bytes 205344 | tf_op jit(solution)/shard_map/all_to_all | solution.py:150
  398.3 7.9 %all-to-all-start.3 = ((f32[401,128,1]{0,2,1:T(1,128)}), f32[401,128,1]{0,2,1:T(1,128)S(1)}, u32[]{:S(2)}, u32[]{:S(2)}) async-start(f32[401,128,1]{0,2,1:T(1,128)} %copy.43), calls=%async_computation.3 | async-start | bytes 524288 | tf_op jit(solution)/shard_map/all_to_all | solution.py:155
  406.3 1.5 multiply_reduce_fusion.5
  407.8 20.0 %all-reduce.10.cloned.1.call-done = f32[400,768]{1,0:T(8,128)} async-done(((f32[400,768]{1,0:T(8,128)}), f32[400,768]{1,0:T(8,128)}) %all-reduce.10.cloned.1.call-update) | async-done | bytes 1228816 | tf_op jit(solution)/shard_map/psum | solution.py:95
  429.1 3.8 collective-permute-start.1
  432.9 1.4 divide_subtract_fusion.3
  434.4 2.5 collective-permute-done.1
  438.0 192.9 %all-reduce.12.cloned.1.call-done = f32[400,768]{1,0:T(8,128)} async-done(((f32[400,768]{1,0:T(8,128)}), f32[400,768]{1,0:T(8,128)}) %all-reduce.12.cloned.1.call-update) | async-done | bytes 1228816 | tf_op jit(solution)/shard_map/psum | solution.py:95
  630.9 1.5 multiply_reduce_fusion
  633.0 1.4 divide_subtract_fusion
  (119 shorter events, 26.6 us)
Async XLA Ops:
  7.2 49.6 %copy-start = (f32[400,768]{1,0:T(8,128)S(1)}, f32[400,768]{1,0:T(8,128)}, u32[]{:S(2)}) copy-start(f32[400,768]{1,0:T(8,128)} %param.18) | copy-start | bytes 3686404
  8.2 40.3 %collective-permute-start = (f32[401,128]{1,0:T(8,128)S(1)}, f32[401,128]{1,0:T(8,128)S(1)}, u32[]{:S(2)}, u32[]{:S(2)}) collective-permute-start(f32[401,128]{1,0:T(8,128)S(1)} %pad_maximum_fusion.2), channel_id=1, source_target_pairs={{0,1},{1,2},{2,3},{3,0},{4,5},{5,6},{6,7},{7,4},{8,9},{9,10},{10,1... | collective-permute-start | bytes 615944 | tf_op jit(solution)/shard_map/ppermute | solution.py:17
  49.4 19.9 %all-to-all-start = ((f32[401,128,1]{0,2,1:T(1,128)}), f32[401,128,1]{0,2,1:T(1,128)}, u32[]{:S(2)}, u32[]{:S(2)}) async-start(f32[401,128,1]{0,2,1:T(1,128)} %copy.35), calls=%async_computation | async-start | bytes 524288 | tf_op jit(solution)/shard_map/all_to_all | solution.py:120
  71.8 11.1 %copy-start.22 = (s32[1,1,1024]{2,1,0:T(1,128)S(1)}, s32[1,1,1024]{2,1,0:T(1,128)}, u32[]{:S(2)}) copy-start(s32[1,1,1024]{2,1,0:T(1,128)} %param.23) | copy-start | bytes 12292
  73.8 21.6 %all-to-all-start.1 = ((f32[401,128,1]{0,2,1:T(1,128)}), f32[401,128,1]{0,2,1:T(1,128)}, u32[]{:S(2)}, u32[]{:S(2)}) async-start(f32[401,128,1]{0,2,1:T(1,128)} %copy.38), calls=%async_computation.1 | async-start | bytes 524288 | tf_op jit(solution)/shard_map/all_to_all | solution.py:124
  82.8 72.2 %all-reduce.6.cloned.1.call-start = ((), (), s32[]{:S(2)}) async-start(), calls=%async_computation.4 | async-start | bytes 2457600 | tf_op jit(solution)/shard_map/psum | solution.py:95
  100.9 4.5 copy-start.9
  102.5 256.1 %all-reduce.8.cloned.1.call-start = ((), (), s32[]{:S(2)}) async-start(), calls=%async_computation.5 | async-start | bytes 2457600 | tf_op jit(solution)/shard_map/psum | solution.py:95
  105.8 2.1 copy-start.17
  105.8 2.1 copy-start.18
  107.9 47.1 %copy-start.24 = (f32[128]{0:T(128)S(1)}, f32[128]{0:T(128)}, u32[]{:S(2)}) copy-start(f32[128]{0:T(128)} %param.15) | copy-start | bytes 1540
  108.2 48.1 %copy-start.25 = (f32[128]{0:T(128)}, f32[128]{0:T(128)S(1)}, u32[]{:S(2)}) copy-start(f32[128]{0:T(128)S(1)} %get-tuple-element.61) | copy-start | bytes 1540
  108.2 48.1 %copy-start.13 = (f32[400,128]{1,0:T(8,128)}, f32[400,128]{1,0:T(8,128)S(1)}, u32[]{:S(2)}) copy-start(f32[400,128]{1,0:T(8,128)S(1)} %get-tuple-element.62) | copy-start | bytes 614404
  108.3 48.1 %copy-start.6 = (f32[400,128]{1,0:T(8,128)S(1)}, f32[400,128]{1,0:T(8,128)}, u32[]{:S(2)}) copy-start(f32[400,128]{1,0:T(8,128)} %param.14) | copy-start | bytes 614404
  155.0 272.8 %all-reduce.10.cloned.1.call-start = ((), (), s32[]{:S(2)}) async-start(), calls=%async_computation.6 | async-start | bytes 2457600 | tf_op jit(solution)/shard_map/psum | solution.py:95
  155.0 205.1 %copy-start.23 = (f32[128]{0:T(128)}, f32[128]{0:T(128)S(1)}, u32[]{:S(2)}) copy-start(f32[128]{0:T(128)S(1)} %sqrt_add_fusion.5) | copy-start | bytes 1540
  156.4 203.7 %copy-start.21 = (f32[768]{0:T(1024)S(1)}, f32[768]{0:T(1024)}, u32[]{:S(2)}) copy-start(f32[768]{0:T(1024)} %param.19) | copy-start | bytes 9220
  361.0 2.9 copy-start.10
  361.0 2.9 copy-start.11
  361.7 2.2 copy-start.5
  368.9 2.4 copy-start.4
  375.0 21.4 %all-to-all-start.2 = ((f32[401,128,1]{0,2,1:T(1,128)}), f32[401,128,1]{0,2,1:T(1,128)S(1)}, u32[]{:S(2)}, u32[]{:S(2)}) async-start(f32[401,128,1]{0,2,1:T(1,128)} %copy.40), calls=%async_computation.2 | async-start | bytes 524288 | tf_op jit(solution)/shard_map/all_to_all | solution.py:150
  397.2 9.1 %copy-start.15 = (bf16[200,512]{1,0:T(8,128)(2,1)S(1)}, bf16[200,512]{1,0:T(8,128)(2,1)}, u32[]{:S(2)}) copy-start(bf16[200,512]{1,0:T(8,128)(2,1)} %get-tuple-element.41) | copy-start | bytes 614404
  397.2 9.1 %copy-start.16 = (bf16[200,512]{1,0:T(8,128)(2,1)S(1)}, bf16[200,512]{1,0:T(8,128)(2,1)}, u32[]{:S(2)}) copy-start(bf16[200,512]{1,0:T(8,128)(2,1)} %get-tuple-element.42) | copy-start | bytes 614404
  398.3 30.7 %all-to-all-start.3 = ((f32[401,128,1]{0,2,1:T(1,128)}), f32[401,128,1]{0,2,1:T(1,128)S(1)}, u32[]{:S(2)}, u32[]{:S(2)}) async-start(f32[401,128,1]{0,2,1:T(1,128)} %copy.43), calls=%async_computation.3 | async-start | bytes 524288 | tf_op jit(solution)/shard_map/all_to_all | solution.py:155
  406.2 224.7 %all-reduce.12.cloned.1.call-start = ((), (), s32[]{:S(2)}) async-start(), calls=%async_computation.7 | async-start | bytes 2457600 | tf_op jit(solution)/shard_map/psum | solution.py:95
  406.3 26.6 %copy-start.7 = (f32[400,128]{1,0:T(8,128)S(1)}, f32[400,128]{1,0:T(8,128)}, u32[]{:S(2)}) copy-start(f32[400,128]{1,0:T(8,128)} %param.14) | copy-start | bytes 614404
  406.3 26.6 %copy-start.14 = (f32[400,128]{1,0:T(8,128)S(1)}, f32[400,128]{1,0:T(8,128)}, u32[]{:S(2)}) copy-start(f32[400,128]{1,0:T(8,128)} %copy-done.13) | copy-start | bytes 614404
  407.8 20.0 %copy-start.26 = (f32[128]{0:T(128)S(1)}, f32[128]{0:T(128)}, u32[]{:S(2)}) copy-start(f32[128]{0:T(128)} %get-tuple-element.65) | copy-start | bytes 1540
  407.8 25.2 %copy-start.19 = (f32[400,128]{1,0:T(8,128)S(1)}, f32[400,128]{1,0:T(8,128)}, u32[]{:S(2)}) copy-start(f32[400,128]{1,0:T(8,128)} %get-tuple-element.66) | copy-start | bytes 614404
  429.1 7.7 %collective-permute-start.1 = (f32[401,128]{1,0:T(8,128)S(1)}, f32[401,128]{1,0:T(8,128)S(1)}, u32[]{:S(2)}, u32[]{:S(2)}) collective-permute-start(f32[401,128]{1,0:T(8,128)S(1)} %bitcast.84), channel_id=1, source_target_pairs={{0,3},{1,0},{2,1},{3,2},{4,7},{5,4},{6,5},{7,6},{8,11},{9,8},{10,9... | collective-permute-start | bytes 615944 | tf_op jit(solution)/shard_map/ppermute | solution.py:17
  630.9 2.1 copy-start.2
  (5 other events, 6.1 us)
Sparse Core Ops, SparseCore 0:
  102.6 52.2 all-reduce.5
  158.6 199.9 all-reduce.7
  374.2 53.4 all-reduce.9
  430.9 199.9 all-reduce.11
